TPU v7x, 32 devices: a whole 2x2x4 slice. The times are simulated.
32 devices in a mesh: shard: 8 (over z, y), tensor: 4 (over x, core).
Axes of the slice: x: 2, y: 2, z: 4, core: 2. Of those that a mesh axis runs over, the one named last changes fastest.
Arguments:
- big_grad: bfloat16 [2, 1280, 768], P(None, 'shard', 'tensor')
- big_weight: bfloat16 [2, 1280, 768], P(None, 'shard', 'tensor'), may hold values from -0.017944336 to 0.017944336
- big_moment: float32 [8, 768, 1280], P('shard', 'tensor'), may hold values from -6 to 6
- small_grad: bfloat16 [2, 1280, 192], P(None, 'shard')
- small_weight: bfloat16 [2, 1280, 192], P(None, 'shard'), may hold values from -0.15625 to 0.15625
- small_moment: float32 [8, 192, 1280], P('shard'), may hold values from -6 to 6
- owners: int32 [2, 2], replicated, may hold values from 0 to 7, as said below
- vec_parts: float32 [8, 2688], P('shard'), may hold values from -0.6 to 0.6
- vec_param: float32 [2688], P('shard'), may hold values from 0.5 to 1.5
- vec_first: float32 [2688], P('shard'), may hold values from -0.6 to 0.6
- vec_second: float32 [2688], P('shard'), may hold values from 0.01 to 1
Outputs:
- big_weight_new: bfloat16 [2, 1280, 768], P(None, 'shard', 'tensor')
- big_moment_new: float32 [8, 768, 1280], P('shard', 'tensor')
- small_weight_new: bfloat16 [2, 1280, 192], P(None, 'shard')
- small_moment_new: float32 [8, 192, 1280], P('shard')
- vec_param_new: float32 [2688], P('shard')
- vec_first_new: float32 [2688], P('shard')
- vec_second_new: float32 [2688], P('shard')
Inputs may be any that keep to these rules, and one draw needn't show every extreme that they name: `owners`: no shard index appears twice in the whole list (over both rows); each aligned group of four shard indices holds exactly one owner of each row; the first and the last shard index own a matrix.
All inputs are finite; a program needn't handle non-finite values.
Results may differ from a plain program's by a relative error of at most 0.0068.
Values may be sent and summed in bfloat16 or wider, within the bound.
A program may use at most 64 MiB of HBM per device.

v0:
```python
import math

import jax
import jax.numpy as jnp
from jax import lax
from jax.sharding import PartitionSpec as P

D = 1280
ITERS = 2


newton_linear = 3.4445
newton_cubic = -4.775
newton_quintic = 2.0315
momentum_rate = 0.95
muon_rate = 0.05
weight_decay = 0.1
norm_epsilon = 1e-07
adam_rate = 0.004
first_decay = 0.9
second_decay = 0.95
adam_epsilon = 1e-08
first_correct = 0.99997343860111
second_correct = 0.99407947077967


def owner_table(owner_list, count):
    devices = lax.broadcasted_iota(jnp.int32, (count, owner_list.shape[0]), 0)
    return (devices == owner_list[None, :]).astype(jnp.bfloat16)


def route_rows(owner_map, pieces):
    flattened = pieces.reshape(pieces.shape[0], -1)
    routed = jnp.dot(owner_map, flattened, preferred_element_type=jnp.float32)
    return routed.astype(jnp.bfloat16).reshape((owner_map.shape[0],) + pieces.shape[1:])


def collect(owner_map, arrived):
    flattened = arrived.reshape(arrived.shape[0], -1)
    picked = lax.dot_general(
        owner_map, flattened, (((0,), (0,)), ((), ())), preferred_element_type=jnp.float32
    )
    return picked.astype(jnp.bfloat16).reshape((owner_map.shape[1],) + arrived.shape[1:])


def advance(arrived, moment, is_owner):
    gradient = arrived.T.astype(jnp.float32)
    renewed = momentum_rate * moment + gradient
    retained = jnp.where(is_owner, renewed, moment)
    blended = jnp.where(is_owner, gradient + momentum_rate * renewed, 0.0).astype(jnp.bfloat16).T
    return (retained, blended)


def normalized(field):
    values = field.astype(jnp.float32)
    squares = jnp.sum(values * values)
    return (values / (jnp.sqrt(squares) + norm_epsilon)).astype(jnp.bfloat16)


def gram_block(left_part, right_part):
    product = lax.dot_general(
        left_part, right_part, (((0,), (0,)), ((), ())), preferred_element_type=jnp.float32
    )
    return product.astype(jnp.bfloat16)


def poly_block(gram_part, gram_full):
    square = jnp.dot(gram_part, gram_full, preferred_element_type=jnp.float32)
    return (newton_cubic * gram_part.astype(jnp.float32) + newton_quintic * square).astype(
        jnp.bfloat16
    )


def newton_step(column_part, full_iterate, polynomial):
    product = lax.dot_general(
        full_iterate, polynomial, (((1,), (1,)), ((), ())), preferred_element_type=jnp.float32
    )
    return (newton_linear * column_part.astype(jnp.float32) + product).astype(jnp.bfloat16)


def small_newton(field):
    iterate = normalized(field)
    for iteration in range(ITERS):
        gram_full = gram_block(iterate, iterate)
        iterate = newton_step(iterate, iterate, poly_block(gram_full, gram_full))
    return iterate


def apply_update(weight, update):
    scale = 0.2 * math.sqrt(D)
    values = weight.astype(jnp.float32)
    return (
        values - muon_rate * (scale * update.astype(jnp.float32) + weight_decay * values)
    ).astype(jnp.bfloat16)


def gather_columns(column_part):
    return lax.all_gather(column_part, "tensor", axis=1, tiled=True)


def gather_gram(gram_part):
    return lax.all_gather(gram_part, "tensor", axis=0, tiled=True)


def per_device(
    big_grad,
    big_weight,
    big_moment,
    small_grad,
    small_weight,
    small_moment,
    owners,
    vec_parts,
    vec_param,
    vec_first,
    vec_second,
):
    shards = lax.axis_size("shard")
    shard_place = lax.axis_index("shard")
    column = lax.axis_index("tensor")
    block_width = big_grad.shape[2]
    rows_dev = big_grad.shape[1]
    matrices = big_grad.shape[0]
    joint_map = owner_table(jnp.concatenate([owners[0], owners[1]]), shards)
    joint_pieces = jnp.concatenate([big_grad, small_grad], axis=0)
    arrived = lax.all_to_all(
        route_rows(joint_map, joint_pieces), "shard", split_axis=0, concat_axis=1, tiled=True
    )[0]
    big_owner = jnp.any(owners[0] == shard_place)
    small_owner = jnp.any(owners[1] == shard_place)
    big_retained, big_blended = advance(arrived, big_moment[0], big_owner)
    small_retained, small_blended = advance(arrived, small_moment[0], small_owner)
    small_result = small_newton(small_blended)
    full_iterate = normalized(gather_columns(big_blended))
    for iteration in range(ITERS):
        owned_part = lax.dynamic_slice_in_dim(full_iterate, column * block_width, block_width, 1)
        gram_full = gather_gram(gram_block(owned_part, full_iterate))
        full_iterate = newton_step(full_iterate, full_iterate, poly_block(gram_full, gram_full))
    big_result = lax.dynamic_slice_in_dim(full_iterate, column * block_width, block_width, 1)
    own_result = jnp.where(big_owner, big_result, small_result)
    returned = lax.all_to_all(
        own_result.reshape(shards, rows_dev, block_width),
        "shard",
        split_axis=0,
        concat_axis=0,
        tiled=True,
    )
    picked = collect(joint_map, returned)
    big_weight_new = apply_update(big_weight, picked[:matrices])
    small_weight_new = apply_update(small_weight, picked[matrices:])
    grad_share = lax.psum_scatter(vec_parts[0], "shard", scatter_dimension=0, tiled=True)
    first_new = first_decay * vec_first + (1.0 - first_decay) * grad_share
    second_new = second_decay * vec_second + (1.0 - second_decay) * grad_share * grad_share
    param_new = vec_param - adam_rate * (first_new / first_correct) / (
        jnp.sqrt(second_new / second_correct) + adam_epsilon
    )
    return (
        big_weight_new,
        big_retained[None],
        small_weight_new,
        small_retained[None],
        param_new,
        first_new,
        second_new,
    )


def solution(mesh):
    return jax.shard_map(
        per_device,
        mesh=mesh,
        in_specs=(
            P(None, "shard", "tensor"),
            P(None, "shard", "tensor"),
            P("shard", "tensor", None),
            P(None, "shard", None),
            P(None, "shard", None),
            P("shard", None, None),
            P(),
            P("shard", None),
            P("shard"),
            P("shard"),
            P("shard"),
        ),
        out_specs=(
            P(None, "shard", "tensor"),
            P("shard", "tensor", None),
            P(None, "shard", None),
            P("shard", None, None),
            P("shard"),
            P("shard"),
            P("shard"),
        ),
        check_vma=False,
    )
```

profile of v0, /device:TPU:0, one launch (start us, length us, event | category | flops | bytes accessed | tf_op | source)
XLA Modules:
  0.0 180.2 jit_solution(17017530316111335332)
XLA Ops:
  7.2 0.8 slice_bitcast_fusion.1
  7.9 1.1 pad_maximum_fusion
  9.0 0.4 reshape.42
  9.4 0.3 convolution_convert_fusion
  9.7 1.6 reshape.43
  11.3 7.3 %all-to-all-start = ((bf16[8,160,192]{2,1,0:T(8,128)(2,1)}), bf16[8,160,192]{2,1,0:T(8,128)(2,1)S(1)}, u32[]{:S(2)}, u32[]{:S(2)}) async-start(bf16[8,160,192]{2,1,0:T(8,128)(2,1)} %reshape.43), calls=%async_computation | async-start | bytes 1310720 | tf_op jit(solution)/shard_map/all_to_all | solution.py:126
  18.7 0.6 compare_reduce_fusion.1
  19.3 16.6 %all-to-all-done = bf16[8,160,192]{2,1,0:T(8,128)(2,1)S(1)} async-done(((bf16[8,160,192]{2,1,0:T(8,128)(2,1)}), bf16[8,160,192]{2,1,0:T(8,128)(2,1)S(1)}, u32[]{:S(2)}, u32[]{:S(2)}) %all-to-all-start) | async-done | bytes 491552 | tf_op jit(solution)/shard_map/all_to_all | solution.py:126
  36.0 0.4 copy.21
  36.4 5.1 %fusion.15 = (f32[1,192,1280]{2,1,0:T(8,128)}, bf16[1280,192]{0,1:T(8,128)(2,1)}, f32[1,192,1280]{2,1,0:T(8,128)}, f32[]{:T(128)}, bf16[192,1280]{1,0:T(8,128)(2,1)}) fusion(f32[1,192,1280]{2,1,0:T(8,128)S(1)} %copy-done.2, f32[1280,192]{0,1:T(8,128)S(1)} %copy.21, pred[]{:T(512)} %get-tuple-element.7, f32[1,192,1280]{2,1,0:T(8,128)} %param.16, ...), kind=kLoop, calls=%fused_computation.37 | loop fusion | flops 4177919 | bytes 5898246 | tf_op jit(solution)/shard_map/broadcast_in_dim | solution.py:159
  41.6 21.0 %all-gather.4.cloned.1.call-done = bf16[1280,768]{0,1:T(8,128)(2,1)} async-done(((bf16[1280,192]{0,1:T(8,128)(2,1)}), bf16[1280,768]{0,1:T(8,128)(2,1)}) %all-gather.4.cloned.1.call-update) | async-done | bytes 1966096 | tf_op jit(solution)/shard_map/all_gather | solution.py:98
  62.6 3.3 %fusion = f32[]{:T(128)} fusion(bf16[1280,768]{0,1:T(8,128)(2,1)} %all-gather.4.cloned.1.call-done), kind=kLoop, calls=%fused_computation.4 | loop fusion | flops 2949119 | bytes 1966084 | tf_op jit(solution)/shard_map/reduce_sum | solution.py:56
  66.6 0.3 fusion.1
  66.9 1.3 copy-done.1
  68.2 1.5 convolution_convert_fusion.3
  69.8 17.6 %all-gather.6.cloned.1.call-done = bf16[768,768]{1,0:T(8,128)(2,1)} async-done(((bf16[192,768]{1,0:T(8,128)(2,1)}), bf16[768,768]{1,0:T(8,128)(2,1)}) %all-gather.6.cloned.1.call-update) | async-done | bytes 1179664 | tf_op jit(solution)/shard_map/all_gather | solution.py:102
  87.4 6.0 %add_convert_fusion = bf16[1280,768]{0,1:T(8,128)(2,1)S(1)} fusion(bf16[1280,768]{0,1:T(8,128)(2,1)} %copy-done.1, bf16[768,768]{1,0:T(8,128)(2,1)} %all-gather.6.cloned.1.call-done), kind=kOutput, calls=%fused_computation.6 | convolution fusion | flops 2422800384 | bytes 5111808 | tf_op jit(solution)/shard_map/dot_general | solution.py:75
  93.5 1.5 convolution_convert_fusion.2
  95.7 0.3 convolution_convert_fusion.5
  96.1 0.4 fusion.2
  96.5 0.3 convolution_convert_fusion.4
  96.8 15.8 %all-gather.8.cloned.1.call-done = bf16[768,768]{1,0:T(8,128)(2,1)} async-done(((bf16[192,768]{1,0:T(8,128)(2,1)}), bf16[768,768]{1,0:T(8,128)(2,1)}) %all-gather.8.cloned.1.call-update) | async-done | bytes 1179664 | tf_op jit(solution)/shard_map/all_gather | solution.py:102
  112.7 6.9 %fusion.20 = f32[1280,768]{0,1:T(8,128)} fusion(bf16[1280,768]{0,1:T(8,128)(2,1)S(1)} %add_convert_fusion, bf16[768,768]{1,0:T(8,128)(2,1)} %all-gather.8.cloned.1.call-done), kind=kOutput, calls=%fused_computation.44 | convolution fusion | flops 2418868224 | bytes 7077888 | tf_op jit(solution)/shard_map/dot_general | solution.py:75
  119.5 2.4 %fusion.4 = bf16[1280,192]{0,1:T(8,128)(2,1)S(1)} fusion(bf16[1280,192]{0,1:T(8,128)(2,1)S(1)} %fusion.2, bf16[192,192]{1,0:T(8,128)(2,1)S(1)} %convolution_convert_fusion.4, f32[1280,768]{0,1:T(8,128)} %fusion.20, s32[]{:T(128)S(6)} %select_n.40, pred[]{:T(512)} %get-tuple-element.7, bf16[1280,768]{0,1:T(8,128)(2,1)S(1)} %add_convert_fusion), kind=kOutput, calls=%fused_computation.11 | convolution fusion | flops 110923776 | bytes 3244037 | tf_op jit(solution)/shard_map/dot_general | solution.py:75
  122.0 1.1 copy.22
  123.0 5.5 %all-to-all-start.1 = ((bf16[8,160,192]{2,1,0:T(8,128)(2,1)}), bf16[8,160,192]{2,1,0:T(8,128)(2,1)S(1)}, u32[]{:S(2)}, u32[]{:S(2)}) async-start(bf16[8,160,192]{2,1,0:T(8,128)(2,1)} %bitcast.8), calls=%async_computation.1 | async-start | bytes 1310720 | tf_op jit(solution)/shard_map/all_to_all | solution.py:141
  128.6 0.6 dynamic-slice
  129.9 40.4 %all-reduce = f32[2688]{0:T(1024)S(1)} all-reduce(f32[2688]{0:T(1024)S(1)} %reduce.1), channel_id=2, replica_groups=mesh['shard'=8,'tensor'=4] {'shard'}, use_global_device_ids=true, to_apply=%region_4.5.clone | all-reduce | flops 2688 | bytes 21504
  170.3 0.7 divide_subtract_fusion
  171.0 0.7 reshape.45
  171.7 0.3 convolution_convert_fusion.1
  172.8 0.8 fusion.26
  (36 shorter events, 1.2 us)
Async XLA Ops:
  9.0 9.7 %copy-start.7 = (s32[2,2]{1,0:T(2,128)S(1)}, s32[2,2]{1,0:T(2,128)}, u32[]{:S(2)}) copy-start(s32[2,2]{1,0:T(2,128)} %param.17) | copy-start | bytes 52
  11.3 24.6 %all-to-all-start = ((bf16[8,160,192]{2,1,0:T(8,128)(2,1)}), bf16[8,160,192]{2,1,0:T(8,128)(2,1)S(1)}, u32[]{:S(2)}, u32[]{:S(2)}) async-start(bf16[8,160,192]{2,1,0:T(8,128)(2,1)} %reshape.43), calls=%async_computation | async-start | bytes 1310720 | tf_op jit(solution)/shard_map/all_to_all | solution.py:126
  18.6 44.0 %all-gather.4.cloned.1.call-start = ((), (), s32[]{:S(2)}) async-start(), calls=%async_computation.2 | async-start | bytes 2457600 | tf_op jit(solution)/shard_map/all_gather | solution.py:98
  19.3 17.1 %copy-start.2 = (f32[1,192,1280]{2,1,0:T(8,128)S(1)}, f32[1,192,1280]{2,1,0:T(8,128)}, u32[]{:S(2)}) copy-start(f32[1,192,1280]{2,1,0:T(8,128)} %param.13) | copy-start | bytes 2949124
  41.5 45.9 %all-gather.6.cloned.1.call-start = ((), (), s32[]{:S(2)}) async-start(), calls=%async_computation.3 | async-start | bytes 1474560 | tf_op jit(solution)/shard_map/all_gather | solution.py:102
  62.6 4.0 %copy-start = (bf16[1280,768]{0,1:T(8,128)(2,1)S(1)}, bf16[1280,768]{0,1:T(8,128)(2,1)}, u32[]{:S(2)}) copy-start(bf16[1280,768]{0,1:T(8,128)(2,1)} %all-gather.4.cloned.1.call-done) | copy-start | bytes 5898244
  66.9 1.3 copy-start.1
  69.8 42.9 %all-gather.8.cloned.1.call-start = ((), (), s32[]{:S(2)}) async-start(), calls=%async_computation.4 | async-start | bytes 1474560 | tf_op jit(solution)/shard_map/all_gather | solution.py:102
  93.5 2.3 %copy-start.3 = (bf16[192,1280]{1,0:T(8,128)(2,1)S(1)}, bf16[192,1280]{1,0:T(8,128)(2,1)}, u32[]{:S(2)}) copy-start(bf16[192,1280]{1,0:T(8,128)(2,1)} %get-tuple-element.19) | copy-start | bytes 1474564
  119.5 9.1 %copy-start.6 = (f32[1,2688]{1,0:T(1,128)S(1)}, f32[1,2688]{1,0:T(1,128)}, u32[]{:S(2)}) copy-start(f32[1,2688]{1,0:T(1,128)} %param.18) | copy-start | bytes 32260
  119.5 9.1 %copy-start.11 = (u32[32]{0:T(128)S(1)}, u32[32]{0:T(128)}, u32[]{:S(2)}) copy-start(u32[32]{0:T(128)} %constant.58) | copy-start | bytes 388
  119.5 50.7 %copy-start.8 = (f32[336]{0:T(512)S(1)}, f32[336]{0:T(512)}, u32[]{:S(2)}) copy-start(f32[336]{0:T(512)} %param.19) | copy-start | bytes 4036
  119.5 50.7 %copy-start.9 = (f32[336]{0:T(512)S(1)}, f32[336]{0:T(512)}, u32[]{:S(2)}) copy-start(f32[336]{0:T(512)} %param.20) | copy-start | bytes 4036
  119.5 50.7 %copy-start.10 = (f32[336]{0:T(512)S(1)}, f32[336]{0:T(512)}, u32[]{:S(2)}) copy-start(f32[336]{0:T(512)} %param.21) | copy-start | bytes 4036
  123.0 47.9 %all-to-all-start.1 = ((bf16[8,160,192]{2,1,0:T(8,128)(2,1)}), bf16[8,160,192]{2,1,0:T(8,128)(2,1)S(1)}, u32[]{:S(2)}, u32[]{:S(2)}) async-start(bf16[8,160,192]{2,1,0:T(8,128)(2,1)} %bitcast.8), calls=%async_computation.1 | async-start | bytes 1310720 | tf_op jit(solution)/shard_map/all_to_all | solution.py:141
  128.6 44.2 %copy-start.4 = (bf16[2,160,192]{2,1,0:T(8,128)(2,1)S(1)}, bf16[2,160,192]{2,1,0:T(8,128)(2,1)}, u32[]{:S(2)}) copy-start(bf16[2,160,192]{2,1,0:T(8,128)(2,1)} %param.12) | copy-start | bytes 368644
  128.6 44.2 %copy-start.5 = (bf16[2,160,192]{2,1,0:T(8,128)(2,1)S(1)}, bf16[2,160,192]{2,1,0:T(8,128)(2,1)}, u32[]{:S(2)}) copy-start(bf16[2,160,192]{2,1,0:T(8,128)(2,1)} %param.15) | copy-start | bytes 368644
Sparse Core Ops, SparseCore 0:
  41.6 20.8 all-gather.3
  69.9 17.4 all-gather.5
  95.2 17.4 all-gather.7
where the time goes:
time: 181 us; the launch traced here: 180 us
  waiting for transfers between devices  71 us (39%)
  blocking collectives  40.4 us (22%)
  matrix products  20.1 us (11%)
  between operations  16 us (9%)
  starting transfers between devices  12.9 us (7%)
  other arithmetic  12.4 us (7%)
  local copies, waits for them, and re-layouts  7.31 us (4%)
    unnamed x1, blocking collectives  40.4 us
    all_gather x2, waiting for transfers between devices, gather_gram(): return lax.all_gather(gram_part, 'tensor', axis=0, tiled=True)  33.4 us
    all_gather x1, waiting for transfers between devices, gather_columns(): return lax.all_gather(column_part, 'tensor', axis=1, tiled=True)  21 us
    all_to_all x1, waiting for transfers between devices, per_device(): lax.all_to_all(route_rows(joint_map, joint_pieces), 'shard', split_axis=0...  16.6 us
    dot_general x4, matrix products, newton_step(): lax.dot_general(full_iterate, polynomial, (((1,), (1,)), ((), ())), prefe...  15.7 us
    all_to_all x1, starting transfers between devices, per_device(): lax.all_to_all(route_rows(joint_map, joint_pieces), 'shard', split_axis=0...  7.28 us
    all_to_all x1, starting transfers between devices, per_device(): lax.all_to_all(own_result.reshape(shards, rows_dev, block_width), 'shard'...  5.52 us
    broadcast_in_dim x1, other arithmetic, per_device(): big_retained[None]  5.05 us
  transfers between devices with their start and end apart: 5, of which 4 were waited for; matrix products, arithmetic and copies ran while one was open for 2% of the time, Pallas kernels for 0%

commit v1 on v0

--- a/solution.py
+++ b/solution.py
@@ -3,6 +3,8 @@
 import jax
 import jax.numpy as jnp
 from jax import lax
+from jax.experimental import pallas as pl
+from jax.experimental.pallas import tpu as pltpu
 from jax.sharding import PartitionSpec as P
 
 D = 1280
@@ -102,7 +104,7 @@
     return lax.all_gather(gram_part, "tensor", axis=0, tiled=True)
 
 
-def per_device(
+def per_device_routed(
     big_grad,
     big_weight,
     big_moment,
@@ -165,9 +167,449 @@
     )
 
 
+ROWS = 160
+BIG_W = 192
+SMALL_W = 48
+BLOCK = BIG_W + SMALL_W
+PART = 80
+LANES = 384
+ORDERS = (("x", "y", "z"), ("y", "z", "x"), ("z", "x", "y"))
+MESH = pl.DeviceIdType.MESH
+
+
+def nt_dot(left, right):
+    return lax.dot_general(left, right, (((1,), (1,)), ((), ())), preferred_element_type=jnp.float32)
+
+
+def trace_of(gram_ref):
+    width = gram_ref.shape[0]
+    step = 64
+    total = jnp.zeros((step, step), jnp.float32)
+    for start in range(0, width, 128):
+        size = min(128, width - start)
+        piece = gram_ref[start : start + size, start : start + size]
+        row = lax.broadcasted_iota(jnp.int32, (size, size), 0)
+        col = lax.broadcasted_iota(jnp.int32, (size, size), 1)
+        kept = jnp.where(row == col, piece, 0.0)
+        total = total + jnp.sum(kept)
+    return total[0:1, 0:1]
+
+
+def first_step(x_ref, gram_f32, gram_ref, poly_ref, out_ref):
+    width = x_ref.shape[0]
+    tile = min(256, width)
+    for n in range(0, width, tile):
+        gram_f32[:, n : n + tile] = nt_dot(x_ref[...], x_ref[n : n + tile, :])
+    squares = trace_of(gram_f32)
+    inverse = 1.0 / (jnp.sqrt(squares) + norm_epsilon)
+    gram_ref[...] = (gram_f32[...] * (inverse * inverse)).astype(jnp.bfloat16)
+    for n in range(0, width, tile):
+        square = jnp.dot(gram_ref[...], gram_ref[:, n : n + tile], preferred_element_type=jnp.float32)
+        poly_ref[:, n : n + tile] = (
+            newton_cubic * gram_ref[:, n : n + tile].astype(jnp.float32) + newton_quintic * square
+        ).astype(jnp.bfloat16)
+    for n in range(0, x_ref.shape[1], 256):
+        product = jnp.dot(poly_ref[...], x_ref[:, n : n + 256], preferred_element_type=jnp.float32)
+        out_ref[:, n : n + 256] = (
+            (newton_linear * x_ref[:, n : n + 256].astype(jnp.float32) + product) * inverse
+        ).astype(jnp.bfloat16)
+
+
+def last_step(x_ref, gram_ref, own, count, main_lanes, rest_lanes):
+    width = x_ref.shape[0]
+    tile = min(256, width)
+    for n in range(0, width, tile):
+        gram_ref[:, n : n + tile] = nt_dot(x_ref[...], x_ref[n : n + tile, :]).astype(jnp.bfloat16)
+    part = gram_ref[own, :]
+    square = jnp.dot(part, gram_ref[...], preferred_element_type=jnp.float32)
+    poly = (newton_cubic * part.astype(jnp.float32) + newton_quintic * square).astype(jnp.bfloat16)
+    results = []
+    for lanes in (main_lanes, rest_lanes):
+        product = jnp.dot(poly, x_ref[:, lanes], preferred_element_type=jnp.float32)
+        results.append(newton_linear * x_ref[own, lanes].astype(jnp.float32) + product)
+    return results
+
+
+def muon_kernel(
+    owners,
+    big_grad,
+    big_weight,
+    big_moment,
+    small_grad,
+    small_weight,
+    small_moment,
+    parts,
+    param,
+    first,
+    second,
+    big_weight_new,
+    big_moment_new,
+    small_weight_new,
+    small_moment_new,
+    param_new,
+    first_new,
+    second_new,
+    grad_rows,
+    grad_out,
+    moment_out,
+    moment_in,
+    blocks,
+    big_x,
+    big_next,
+    small_x,
+    small_next,
+    big_gram_f32,
+    big_gram,
+    big_poly,
+    small_gram_f32,
+    small_gram,
+    small_poly,
+    result_rows,
+    result_in,
+    parts_in,
+    swap_sem,
+    moment_sem,
+    stage_send,
+    stage_recv,
+    pair_send,
+    pair_recv,
+    own_sem,
+    back_sem,
+    vec_send,
+    vec_recv,
+):
+    shard = lax.axis_index("shard")
+    tensor = lax.axis_index("tensor")
+    group = shard // 4
+    place = shard % 4
+    z, y = place // 2, shard % 2
+    x, core = tensor // 2, tensor % 2
+    partner = {"shard": (shard + 4) % 8, "tensor": tensor}
+    sibling = {"shard": shard, "tensor": x * 2 + (1 - core)}
+    neighbour = {
+        "x": {"shard": shard, "tensor": (1 - x) * 2 + core},
+        "y": {"shard": group * 4 + z * 2 + (1 - y), "tensor": tensor},
+        "z": {"shard": group * 4 + (1 - z) * 2 + y, "tensor": tensor},
+    }
+
+    barrier = pltpu.get_barrier_semaphore()
+    for k in range(1, 8):
+        pl.semaphore_signal(
+            barrier, inc=1, device_id={"shard": (shard + k) % 8, "tensor": tensor}, device_id_type=MESH
+        )
+    for peer in (neighbour["x"], sibling):
+        pl.semaphore_signal(barrier, inc=1, device_id=peer, device_id_type=MESH)
+
+    first_is_mine = jnp.where(owners[0, 0] >= 4, 1, 0) == group
+    small_is_mine = jnp.where(owners[1, 0] >= 4, 1, 0) == group
+    big_owner = lax.rem(jnp.where(first_is_mine, owners[0, 0], owners[0, 1]), 4)
+    small_owner = lax.rem(jnp.where(small_is_mine, owners[1, 0], owners[1, 1]), 4)
+
+    def columns(index):
+        big = jnp.where(first_is_mine == (index == 0), big_grad[0].astype(jnp.float32), big_grad[1].astype(jnp.float32))
+        small = jnp.where(
+            small_is_mine == (index == 0), small_grad[0].astype(jnp.float32), small_grad[1].astype(jnp.float32)
+        )
+        picked = small[:, 0:SMALL_W]
+        for k in range(1, 4):
+            picked = jnp.where(tensor == k, small[:, k * SMALL_W : (k + 1) * SMALL_W], picked)
+        filler = jnp.zeros((ROWS, 256 - BLOCK), jnp.float32)
+        return jnp.concatenate([big, picked, filler], axis=1).astype(jnp.bfloat16)
+
+    grad_out[...] = columns(1)
+    pl.semaphore_wait(barrier, 9)
+    own_rows = pl.ds(pl.multiple_of(group * ROWS, ROWS), ROWS)
+    other_rows = pl.ds(pl.multiple_of((1 - group) * ROWS, ROWS), ROWS)
+    swap = pltpu.make_async_remote_copy(
+        grad_out, grad_rows.at[own_rows], swap_sem.at[0], swap_sem.at[1], device_id=partner, device_id_type=MESH
+    )
+    swap.start()
+
+    moment = jnp.concatenate(
+        [big_moment[0], small_moment[0, pl.ds(pl.multiple_of(tensor * SMALL_W, SMALL_W), SMALL_W), :]], axis=0
+    )
+    for j in range(4):
+        moment_out[j] = jnp.concatenate(
+            [
+                moment[:, j * ROWS : (j + 1) * ROWS],
+                moment[:, (j + 4) * ROWS : (j + 5) * ROWS],
+                jnp.zeros((BLOCK, LANES - 2 * ROWS), jnp.float32),
+            ],
+            axis=1,
+        ).astype(jnp.bfloat16)
+    moves = []
+    for k in (3, 2, 1):
+        there = (place + k) % 4
+        moves.append(
+            pltpu.make_async_remote_copy(
+                moment_out.at[there],
+                moment_in.at[place],
+                moment_sem.at[0, k],
+                moment_sem.at[1, k],
+                device_id={"shard": group * 4 + there, "tensor": tensor},
+                device_id_type=MESH,
+            )
+        )
+        moves[-1].start()
+    vec_moves = []
+    for k in range(1, 8):
+        there = (shard + k) % 8
+        vec_moves.append(
+            pltpu.make_async_remote_copy(
+                parts.at[there],
+                parts_in.at[k],
+                vec_send.at[k],
+                vec_recv.at[k],
+                device_id={"shard": there, "tensor": tensor},
+                device_id_type=MESH,
+            )
+        )
+        vec_moves[-1].start()
+    moment_in[place] = moment_out[place]
+    grad_rows[own_rows, :] = columns(0)
+    grad_rows[2 * ROWS :, :] = jnp.zeros((LANES - 2 * ROWS, 256), jnp.bfloat16)
+    swap.wait_recv()
+    gradient = grad_rows[...].astype(jnp.float32).T[:BLOCK]
+    for move in moves:
+        move.wait_recv()
+    previous = jnp.concatenate([moment_in[big_owner, :BIG_W, :], moment_in[small_owner, BIG_W:, :]], axis=0)
+    renewed = momentum_rate * previous.astype(jnp.float32) + gradient
+    blended = gradient + momentum_rate * renewed
+    rest = blended[:, 256:]
+    rest = jnp.where(y == 0, rest, pltpu.roll(rest, 64, 1))
+    blocks[z, y, x, core, :, 0:256] = blended[:, :256].astype(jnp.bfloat16)
+    blocks[z, y, x, core, :, 256:] = rest.astype(jnp.bfloat16)
+
+    here = {"x": x, "y": y, "z": z}
+
+    def region(p, k, received):
+        done = ORDERS[p][:k]
+        index = []
+        for name in ("z", "y", "x"):
+            if name in done:
+                index.append(slice(None))
+            elif received and name == ORDERS[p][k]:
+                index.append(1 - here[name])
+            else:
+                index.append(here[name])
+        return blocks.at[index[0], index[1], index[2], core, p * PART : (p + 1) * PART]
+
+    def stage(p, k):
+        ref = region(p, k, False)
+        return pltpu.make_async_remote_copy(
+            ref,
+            ref,
+            stage_send.at[p, k],
+            stage_recv.at[p, k],
+            device_id=neighbour[ORDERS[p][k]],
+            device_id_type=MESH,
+        )
+
+    def forward(p, k):
+        ref = region(p, k, True)
+        return pltpu.make_async_remote_copy(
+            ref, ref, pair_send.at[p, k], pair_recv.at[p, k], device_id=sibling, device_id_type=MESH
+        )
+
+    sent = []
+    for p in range(3):
+        copy = stage(p, 0)
+        copy.start()
+        sent.append(copy)
+    own_ref = blocks.at[z, y, x, core]
+    own_copy = pltpu.make_async_remote_copy(
+        own_ref, own_ref, own_sem.at[0], own_sem.at[1], device_id=sibling, device_id_type=MESH
+    )
+    own_copy.start()
+    forwarded = []
+    for k in range(3):
+        for p in range(3):
+            sent[3 * k + p].wait_recv()
+            if k < 2:
+                copy = stage(p, k + 1)
+                copy.start()
+                sent.append(copy)
+            copy = forward(p, k)
+            copy.start()
+            forwarded.append(copy)
+    own_copy.wait_recv()
+    for copy in forwarded:
+        copy.wait_recv()
+
+    for a in range(2):
+        for b in range(2):
+            lanes = slice((2 * a + b) * 256, (2 * a + b + 1) * 256)
+            for t in range(4):
+                big_x[t * BIG_W : (t + 1) * BIG_W, lanes] = blocks[a, b, t // 2, t % 2, :BIG_W, :256]
+                small_x[t * SMALL_W : (t + 1) * SMALL_W, lanes] = blocks[a, b, t // 2, t % 2, BIG_W:, :256]
+        lanes = slice(1024 + a * 128, 1024 + (a + 1) * 128)
+        for t in range(4):
+            both = blocks[a, 0, t // 2, t % 2, :, 256:] + blocks[a, 1, t // 2, t % 2, :, 256:]
+            big_x[t * BIG_W : (t + 1) * BIG_W, lanes] = both[:BIG_W]
+            small_x[t * SMALL_W : (t + 1) * SMALL_W, lanes] = both[BIG_W:]
+
+    first_step(small_x, small_gram_f32, small_gram, small_poly, small_next)
+    first_step(big_x, big_gram_f32, big_gram, big_poly, big_next)
+    main_lanes = pl.ds(pl.multiple_of(place * 256, 256), 256)
+    rest_lanes = pl.ds(pl.multiple_of(1024 + z * 128, 128), 128)
+    small_main, small_rest = last_step(
+        small_next, small_gram, slice(None), 4 * SMALL_W, main_lanes, rest_lanes
+    )
+    own_columns = pl.ds(pl.multiple_of(tensor * BIG_W, BIG_W), BIG_W)
+    big_main, big_rest = last_step(big_next, big_gram, own_columns, BIG_W, main_lanes, rest_lanes)
+    main = jnp.concatenate([big_main, small_main], axis=0)
+    rest = jnp.concatenate([big_rest, small_rest], axis=0)
+    rest = jnp.where(y == 0, rest, pltpu.roll(rest, 64, 1))
+    result_rows[0:256, :] = main.T.astype(jnp.bfloat16)
+    result_rows[256:LANES, :] = rest.T.astype(jnp.bfloat16)
+    back = pltpu.make_async_remote_copy(
+        result_rows.at[other_rows], result_in, back_sem.at[0], back_sem.at[1], device_id=partner, device_id_type=MESH
+    )
+    back.start()
+
+    share = parts[shard]
+    for k in range(1, 8):
+        vec_moves[k - 1].wait_recv()
+        share = share + parts_in[k]
+    first_value = first_decay * first[...] + (1.0 - first_decay) * share
+    second_value = second_decay * second[...] + (1.0 - second_decay) * share * share
+    first_new[...] = first_value
+    second_new[...] = second_value
+    param_new[...] = param[...] - adam_rate * (first_value / first_correct) / (
+        jnp.sqrt(second_value / second_correct) + adam_epsilon
+    )
+
+    from_blended = 1.0 / (1.0 + momentum_rate)
+    from_moment = momentum_rate - momentum_rate * momentum_rate / (1.0 + momentum_rate)
+
+    def row_order(load):
+        low, high = [], []
+        for j in range(4):
+            main = load(j // 2, j % 2, slice(0, 256)).astype(jnp.float32)
+            rest = load(j // 2, j % 2, slice(256, LANES)).astype(jnp.float32)
+            if j % 2 == 1:
+                rest = pltpu.roll(rest, 64, 1)
+            low.append(main[:, :ROWS])
+            high.append(jnp.concatenate([main[:, ROWS:], rest[:, :64]], axis=1))
+        return jnp.concatenate(low + high, axis=1)
+
+    def small_block(a, b, lanes):
+        return jnp.concatenate([blocks[a, b, t // 2, t % 2, BIG_W:, lanes] for t in range(4)], axis=0)
+
+    big_blended = row_order(lambda a, b, lanes: blocks[a, b, x, core, :BIG_W, lanes])
+    big_moment_new[0] = jnp.where(
+        big_owner == place, from_blended * big_blended + from_moment * big_moment[0], big_moment[0]
+    )
+    small_blended = row_order(small_block)
+    small_moment_new[0] = jnp.where(
+        small_owner == place, from_blended * small_blended + from_moment * small_moment[0], small_moment[0]
+    )
+
+    back.wait_recv()
+    mine = result_rows[own_rows, :]
+    others = result_in[...]
+    scale = 0.2 * math.sqrt(D)
+    for index in range(2):
+        for weight, out, lanes, is_mine in (
+            (big_weight, big_weight_new, slice(0, BIG_W), first_is_mine),
+            (small_weight, small_weight_new, slice(BIG_W, 2 * BIG_W), small_is_mine),
+        ):
+            update = jnp.where(
+                is_mine == (index == 0), mine[:, lanes].astype(jnp.float32), others[:, lanes].astype(jnp.float32)
+            )
+            values = weight[index].astype(jnp.float32)
+            out[index] = (values - muon_rate * (scale * update + weight_decay * values)).astype(jnp.bfloat16)
+    for copy in [swap, own_copy, back] + moves + vec_moves + sent + forwarded:
+        copy.wait_send()
+
+
+def per_device(
+    big_grad,
+    big_weight,
+    big_moment,
+    small_grad,
+    small_weight,
+    small_moment,
+    owners,
+    vec_parts,
+    vec_param,
+    vec_first,
+    vec_second,
+):
+    entries = vec_param.shape[0]
+    shards = lax.axis_size("shard")
+    vmem = pl.BlockSpec(memory_space=pltpu.VMEM)
+    rows = jax.ShapeDtypeStruct((1, entries), jnp.float32)
+    out_shape = (
+        jax.ShapeDtypeStruct(big_weight.shape, jnp.bfloat16),
+        jax.ShapeDtypeStruct(big_moment.shape, jnp.float32),
+        jax.ShapeDtypeStruct(small_weight.shape, jnp.bfloat16),
+        jax.ShapeDtypeStruct(small_moment.shape, jnp.float32),
+        rows,
+        rows,
+        rows,
+    )
+    bf16, f32 = jnp.bfloat16, jnp.float32
+    big, small = 4 * BIG_W, 4 * SMALL_W
+    dma = pltpu.SemaphoreType.DMA
+    outs = pl.pallas_call(
+        muon_kernel,
+        out_shape=out_shape,
+        in_specs=[pl.BlockSpec(memory_space=pltpu.SMEM)] + [vmem] * 10,
+        out_specs=(vmem,) * 7,
+        scratch_shapes=[
+            pltpu.VMEM((LANES, 256), bf16),
+            pltpu.VMEM((ROWS, 256), bf16),
+            pltpu.VMEM((4, BLOCK, LANES), bf16),
+            pltpu.VMEM((4, BLOCK, LANES), bf16),
+            pltpu.VMEM((2, 2, 2, 2, BLOCK, LANES), bf16),
+            pltpu.VMEM((big, D), bf16),
+            pltpu.VMEM((big, D), bf16),
+            pltpu.VMEM((small, D), bf16),
+            pltpu.VMEM((small, D), bf16),
+            pltpu.VMEM((big, big), f32),
+            pltpu.VMEM((big, big), bf16),
+            pltpu.VMEM((big, big), bf16),
+            pltpu.VMEM((small, small), f32),
+            pltpu.VMEM((small, small), bf16),
+            pltpu.VMEM((small, small), bf16),
+            pltpu.VMEM((LANES, LANES), bf16),
+            pltpu.VMEM((ROWS, LANES), bf16),
+            pltpu.VMEM((shards, 1, entries), f32),
+            dma((2,)),
+            dma((2, 4)),
+            dma((3, 3)),
+            dma((3, 3)),
+            dma((3, 3)),
+            dma((3, 3)),
+            dma((2,)),
+            dma((2,)),
+            dma((8,)),
+            dma((8,)),
+        ],
+        compiler_params=pltpu.CompilerParams(
+            collective_id=0, has_side_effects=True, vmem_limit_bytes=48 * 1024 * 1024
+        ),
+    )(
+        owners,
+        big_grad,
+        big_weight,
+        big_moment,
+        small_grad,
+        small_weight,
+        small_moment,
+        vec_parts.reshape(shards, 1, entries),
+        vec_param.reshape(1, entries),
+        vec_first.reshape(1, entries),
+        vec_second.reshape(1, entries),
+    )
+    return tuple(outs[:4]) + tuple(value.reshape(entries) for value in outs[4:])
+
+
 def solution(mesh):
+    grouped = mesh.shape["shard"] == 8 and mesh.shape["tensor"] == 4
     return jax.shard_map(
-        per_device,
+        per_device if grouped else per_device_routed,
         mesh=mesh,
         in_specs=(
             P(None, "shard", "tensor"),

time: 181 us -> 65.2 us (0.36)
  waiting for transfers between devices: 71 us -> 0 us
  Pallas kernels: 0 us -> 49.4 us
  blocking collectives: 40.4 us -> 0 us
  matrix products: 20.1 us -> 0 us
  between operations: 16 us -> 0.67 us
  starting transfers between devices: 12.9 us -> 0 us
  other arithmetic: 12.4 us -> 2.52 us
  local copies, waits for them, and re-layouts: 7.31 us -> 12 us
    all_gather x3 -> x0, waiting for transfers between devices: 54.4 us -> none  [the longest x2 33.4 us: gather_gram(): return lax.all_gather(gram_part, 'tensor', axis=0, tiled=True)]
    pallas_call x0 -> x1, Pallas kernels: none -> 49.4 us  [per_device(): pl.pallas_call(muon_kernel, out_shape=out_shape, in_specs=[pl.BlockSpec(m...]
    unnamed x1 -> x0, blocking collectives: 40.4 us -> none
    dot_general x10 -> x0, matrix products: 20.1 us -> none  [the longest x4 15.7 us: newton_step(): lax.dot_general(full_iterate, polynomial, (((1,), (1,)), ((), ())), prefe...]
    all_to_all x2 -> x0, waiting for transfers between devices: 16.6 us -> none  [the longest x1 16.6 us: per_device(): lax.all_to_all(route_rows(joint_map, joint_pieces), 'shard', split_axis=0...]
    all_to_all x2 -> x0, starting transfers between devices: 12.8 us -> none  [the longest x1 7.28 us: per_device(): lax.all_to_all(route_rows(joint_map, joint_pieces), 'shard', split_axis=0...]
    unnamed x25 -> x24, local copies, waits for them, and re-layouts: 1.93 us -> 11.9 us
    broadcast_in_dim x1 -> x0, other arithmetic: 5.05 us -> none  [per_device(): big_retained[None]]
  transfers between devices with their start and end apart: 5 -> 0, of which waited for: 4 -> 0; matrix products, arithmetic and copies ran while one was open for 2% -> 0% of each run, Pallas kernels for 0% -> 0%
where the time goes in v1:
time: 65.2 us; the launch traced here: 64.6 us
  Pallas kernels  49.4 us (76%)
  local copies, waits for them, and re-layouts  12 us (18%)
  other arithmetic  2.52 us (4%)
  between operations  0.67 us (1%)
    pallas_call x1, Pallas kernels, per_device(): pl.pallas_call(muon_kernel, out_shape=out_shape, in_specs=[pl.BlockSpec(m...  49.4 us
    unnamed x24, local copies, waits for them, and re-layouts  11.9 us
    pallas_call x3, other arithmetic, per_device(): pl.pallas_call(muon_kernel, out_shape=out_shape, in_specs=[pl.BlockSpec(m...  1.79 us

profile of v1, /device:TPU:0, one launch (start us, length us, event | category | flops | bytes accessed | tf_op | source)
XLA Modules:
  0.0 64.6 jit_solution(2417950143794762690)
XLA Ops:
  0.6 0.7 %reduce = f32[2688]{0:T(1024)S(1)} reduce(f32[1,2688]{1,0:T(1,128)} %param.18, f32[]{:T(128)} %constant.3), dimensions={0}, to_apply=%param.18.reduce_sub_computation | reduce | bytes 21508 | tf_op args[7]
  1.4 0.0 copy-start.7
  1.4 0.1 reshape.35.parts
  1.5 0.6 copy-done.7
  2.1 0.0 copy-start.8
  2.1 0.7 %copy-done.8 = f32[336]{0:T(512)S(1)} copy-done((f32[336]{0:T(512)S(1)}, f32[336]{0:T(512)}, u32[]{:S(2)}) %copy-start.8) | copy-done | bytes 1368
  2.7 0.0 copy-start.9
  2.7 0.7 %copy-done.9 = f32[336]{0:T(512)S(1)} copy-done((f32[336]{0:T(512)S(1)}, f32[336]{0:T(512)}, u32[]{:S(2)}) %copy-start.9) | copy-done | bytes 1368
  3.4 0.0 copy-start.6
  3.4 0.7 %copy-done.6 = s32[2,2]{1,0:T(2,128)S(1)} copy-done((s32[2,2]{1,0:T(2,128)S(1)}, s32[2,2]{1,0:T(2,128)}, u32[]{:S(2)}) %copy-start.6) | copy-done | bytes 40
  4.1 0.0 copy-start
  4.1 1.2 %copy-done = f32[1,192,1280]{2,1,0:T(8,128)S(1)} copy-done((f32[1,192,1280]{2,1,0:T(8,128)S(1)}, f32[1,192,1280]{2,1,0:T(8,128)}, u32[]{:S(2)}) %copy-start) | copy-done | bytes 983064
  5.3 0.0 copy-start.1
  5.3 1.2 %copy-done.1 = f32[1,192,1280]{2,1,0:T(8,128)S(1)} copy-done((f32[1,192,1280]{2,1,0:T(8,128)S(1)}, f32[1,192,1280]{2,1,0:T(8,128)}, u32[]{:S(2)}) %copy-start.1) | copy-done | bytes 983064
  6.5 0.0 copy-start.2
  6.5 0.9 %copy-done.2 = bf16[2,160,192]{2,1,0:T(8,128)(2,1)S(1)} copy-done((bf16[2,160,192]{2,1,0:T(8,128)(2,1)S(1)}, bf16[2,160,192]{2,1,0:T(8,128)(2,1)}, u32[]{:S(2)}) %copy-start.2) | copy-done | bytes 122904
  7.4 0.0 copy-start.3
  7.4 0.9 %copy-done.3 = bf16[2,160,192]{2,1,0:T(8,128)(2,1)S(1)} copy-done((bf16[2,160,192]{2,1,0:T(8,128)(2,1)S(1)}, bf16[2,160,192]{2,1,0:T(8,128)(2,1)}, u32[]{:S(2)}) %copy-start.3) | copy-done | bytes 122904
  8.3 0.0 copy-start.4
  8.3 0.9 %copy-done.4 = bf16[2,160,192]{2,1,0:T(8,128)(2,1)S(1)} copy-done((bf16[2,160,192]{2,1,0:T(8,128)(2,1)S(1)}, bf16[2,160,192]{2,1,0:T(8,128)(2,1)}, u32[]{:S(2)}) %copy-start.4) | copy-done | bytes 122904
  9.3 0.0 copy-start.5
  9.3 0.9 %copy-done.5 = bf16[2,160,192]{2,1,0:T(8,128)(2,1)S(1)} copy-done((bf16[2,160,192]{2,1,0:T(8,128)(2,1)S(1)}, bf16[2,160,192]{2,1,0:T(8,128)(2,1)}, u32[]{:S(2)}) %copy-start.5) | copy-done | bytes 122904
  10.2 49.4 %shard_map.162 = (bf16[2,160,192]{2,1,0:T(8,128)(2,1)S(1)}, f32[1,192,1280]{2,1,0:T(8,128)S(1)}, bf16[2,160,192]{2,1,0:T(8,128)(2,1)S(1)}, f32[1,192,1280]{2,1,0...) custom-call(s32[2,2]{1,0:T(2,128)S(1)} %copy-done.6, ...), custom_call_target="tpu_custom_call" | custom-call | tf_op jit(solution)/shard_map/pallas_call | solution.py:555
  59.6 0.6 reduce.1
  60.2 0.6 reduce.2
  60.8 0.6 reduce.3
  61.4 0.7 %copy.22 = bf16[2,160,192]{2,1,0:T(8,128)(2,1)} copy(bf16[2,160,192]{2,1,0:T(8,128)(2,1)S(1)} %get-tuple-element.28) | data formatting | bytes 245760
  62.1 0.9 %copy.23 = f32[1,192,1280]{2,1,0:T(8,128)} copy(f32[1,192,1280]{2,1,0:T(8,128)S(1)} %get-tuple-element.29) | data formatting | bytes 1966080
  63.0 0.7 %copy.24 = bf16[2,160,192]{2,1,0:T(8,128)(2,1)} copy(bf16[2,160,192]{2,1,0:T(8,128)(2,1)S(1)} %get-tuple-element.30) | data formatting | bytes 245760
  63.7 0.9 %copy.25 = f32[1,192,1280]{2,1,0:T(8,128)} copy(f32[1,192,1280]{2,1,0:T(8,128)S(1)} %get-tuple-element.31) | data formatting | bytes 1966080
  (3 shorter events, 0.0 us)
Async XLA Ops:
  1.4 0.7 %copy-start.7 = (f32[336]{0:T(512)S(1)}, f32[336]{0:T(512)}, u32[]{:S(2)}) copy-start(f32[336]{0:T(512)} %param.19) | copy-start | bytes 4036
  2.1 0.7 %copy-start.8 = (f32[336]{0:T(512)S(1)}, f32[336]{0:T(512)}, u32[]{:S(2)}) copy-start(f32[336]{0:T(512)} %param.20) | copy-start | bytes 4036
  2.7 0.7 %copy-start.9 = (f32[336]{0:T(512)S(1)}, f32[336]{0:T(512)}, u32[]{:S(2)}) copy-start(f32[336]{0:T(512)} %param.21) | copy-start | bytes 4036
  3.4 0.7 %copy-start.6 = (s32[2,2]{1,0:T(2,128)S(1)}, s32[2,2]{1,0:T(2,128)}, u32[]{:S(2)}) copy-start(s32[2,2]{1,0:T(2,128)} %owners.1) | copy-start | bytes 52
  4.1 1.2 %copy-start = (f32[1,192,1280]{2,1,0:T(8,128)S(1)}, f32[1,192,1280]{2,1,0:T(8,128)}, u32[]{:S(2)}) copy-start(f32[1,192,1280]{2,1,0:T(8,128)} %big_moment.1) | copy-start | bytes 2949124
  5.3 1.2 %copy-start.1 = (f32[1,192,1280]{2,1,0:T(8,128)S(1)}, f32[1,192,1280]{2,1,0:T(8,128)}, u32[]{:S(2)}) copy-start(f32[1,192,1280]{2,1,0:T(8,128)} %small_moment.1) | copy-start | bytes 2949124
  6.5 0.9 %copy-start.2 = (bf16[2,160,192]{2,1,0:T(8,128)(2,1)S(1)}, bf16[2,160,192]{2,1,0:T(8,128)(2,1)}, u32[]{:S(2)}) copy-start(bf16[2,160,192]{2,1,0:T(8,128)(2,1)} %big_grad.1) | copy-start | bytes 368644
  7.4 0.9 %copy-start.3 = (bf16[2,160,192]{2,1,0:T(8,128)(2,1)S(1)}, bf16[2,160,192]{2,1,0:T(8,128)(2,1)}, u32[]{:S(2)}) copy-start(bf16[2,160,192]{2,1,0:T(8,128)(2,1)} %big_weight.1) | copy-start | bytes 368644
  8.3 0.9 %copy-start.4 = (bf16[2,160,192]{2,1,0:T(8,128)(2,1)S(1)}, bf16[2,160,192]{2,1,0:T(8,128)(2,1)}, u32[]{:S(2)}) copy-start(bf16[2,160,192]{2,1,0:T(8,128)(2,1)} %small_grad.1) | copy-start | bytes 368644
  9.3 0.9 %copy-start.5 = (bf16[2,160,192]{2,1,0:T(8,128)(2,1)S(1)}, bf16[2,160,192]{2,1,0:T(8,128)(2,1)}, u32[]{:S(2)}) copy-start(bf16[2,160,192]{2,1,0:T(8,128)(2,1)} %small_weight.1) | copy-start | bytes 368644

commit v2 on v1

--- a/solution.py
+++ b/solution.py
@@ -171,7 +171,9 @@
 BIG_W = 192
 SMALL_W = 48
 BLOCK = BIG_W + SMALL_W
-PART = 80
+REST = 64
+PACKED = BLOCK + REST
+PARTS = ((0, 112), (112, 96), (208, 96))
 LANES = 384
 ORDERS = (("x", "y", "z"), ("y", "z", "x"), ("z", "x", "y"))
 MESH = pl.DeviceIdType.MESH
@@ -230,15 +232,21 @@
     return results
 
 
+def pack(block):
+    groups = [block[k * REST : (k + 1) * REST, 256:320] for k in range(3)]
+    groups.append(jnp.concatenate([block[BIG_W:, 256:320], jnp.zeros((REST - SMALL_W, 64), jnp.float32)], axis=0))
+    return jnp.concatenate([block[:, :256], jnp.concatenate(groups, axis=1)], axis=0)
+
+
 def muon_kernel(
     owners,
-    big_grad,
-    big_weight,
-    big_moment,
-    small_grad,
-    small_weight,
-    small_moment,
-    parts,
+    big_grad_hbm,
+    big_weight_hbm,
+    big_moment_hbm,
+    small_grad_hbm,
+    small_weight_hbm,
+    small_moment_hbm,
+    parts_hbm,
     param,
     first,
     second,
@@ -249,6 +257,14 @@
     param_new,
     first_new,
     second_new,
+    big_grad,
+    big_weight,
+    big_moment,
+    small_grad,
+    small_weight,
+    small_moment,
+    parts,
+    load_sem,
     grad_rows,
     grad_out,
     moment_out,
@@ -266,6 +282,8 @@
     small_poly,
     result_rows,
     result_in,
+    small_rows,
+    small_in,
     parts_in,
     swap_sem,
     moment_sem,
@@ -278,6 +296,22 @@
     vec_send,
     vec_recv,
 ):
+    loads = [
+        pltpu.make_async_copy(source, target, load_sem.at[k])
+        for k, (source, target) in enumerate(
+            (
+                (big_grad_hbm, big_grad),
+                (small_grad_hbm, small_grad),
+                (big_moment_hbm, big_moment),
+                (small_moment_hbm, small_moment),
+                (parts_hbm, parts),
+                (big_weight_hbm, big_weight),
+                (small_weight_hbm, small_weight),
+            )
+        )
+    ]
+    for copy in loads:
+        copy.start()
     shard = lax.axis_index("shard")
     tensor = lax.axis_index("tensor")
     group = shard // 4
@@ -316,6 +350,8 @@
         filler = jnp.zeros((ROWS, 256 - BLOCK), jnp.float32)
         return jnp.concatenate([big, picked, filler], axis=1).astype(jnp.bfloat16)
 
+    loads[0].wait()
+    loads[1].wait()
     grad_out[...] = columns(1)
     pl.semaphore_wait(barrier, 9)
     own_rows = pl.ds(pl.multiple_of(group * ROWS, ROWS), ROWS)
@@ -325,18 +361,16 @@
     )
     swap.start()
 
+    loads[2].wait()
+    loads[3].wait()
     moment = jnp.concatenate(
         [big_moment[0], small_moment[0, pl.ds(pl.multiple_of(tensor * SMALL_W, SMALL_W), SMALL_W), :]], axis=0
     )
     for j in range(4):
-        moment_out[j] = jnp.concatenate(
-            [
-                moment[:, j * ROWS : (j + 1) * ROWS],
-                moment[:, (j + 4) * ROWS : (j + 5) * ROWS],
-                jnp.zeros((BLOCK, LANES - 2 * ROWS), jnp.float32),
-            ],
-            axis=1,
-        ).astype(jnp.bfloat16)
+        rows = jnp.concatenate(
+            [moment[:, j * ROWS : (j + 1) * ROWS], moment[:, (j + 4) * ROWS : (j + 5) * ROWS]], axis=1
+        )
+        moment_out[j] = pack(rows).astype(jnp.bfloat16)
     moves = []
     for k in (3, 2, 1):
         there = (place + k) % 4
@@ -351,6 +385,7 @@
             )
         )
         moves[-1].start()
+    loads[4].wait()
     vec_moves = []
     for k in range(1, 8):
         there = (shard + k) % 8
@@ -369,16 +404,22 @@
     grad_rows[own_rows, :] = columns(0)
     grad_rows[2 * ROWS :, :] = jnp.zeros((LANES - 2 * ROWS, 256), jnp.bfloat16)
     swap.wait_recv()
-    gradient = grad_rows[...].astype(jnp.float32).T[:BLOCK]
+    gradient = pack(grad_rows[...].astype(jnp.float32).T[:BLOCK])
     for move in moves:
         move.wait_recv()
-    previous = jnp.concatenate([moment_in[big_owner, :BIG_W, :], moment_in[small_owner, BIG_W:, :]], axis=0)
-    renewed = momentum_rate * previous.astype(jnp.float32) + gradient
-    blended = gradient + momentum_rate * renewed
-    rest = blended[:, 256:]
-    rest = jnp.where(y == 0, rest, pltpu.roll(rest, 64, 1))
-    blocks[z, y, x, core, :, 0:256] = blended[:, :256].astype(jnp.bfloat16)
-    blocks[z, y, x, core, :, 256:] = rest.astype(jnp.bfloat16)
+    low = moment_in[big_owner, BLOCK:, :]
+    high = moment_in[small_owner, BLOCK:, :]
+    lane = lax.broadcasted_iota(jnp.int32, (REST, 256), 1)
+    previous = jnp.concatenate(
+        [
+            moment_in[big_owner, :BIG_W, :].astype(jnp.float32),
+            moment_in[small_owner, BIG_W:BLOCK, :].astype(jnp.float32),
+            jnp.where(lane < BIG_W, low.astype(jnp.float32), high.astype(jnp.float32)),
+        ],
+        axis=0,
+    )
+    renewed = momentum_rate * previous + gradient
+    blocks[z, y, x, core] = (gradient + momentum_rate * renewed).astype(jnp.bfloat16)
 
     here = {"x": x, "y": y, "z": z}
 
@@ -392,7 +433,7 @@
                 index.append(1 - here[name])
             else:
                 index.append(here[name])
-        return blocks.at[index[0], index[1], index[2], core, p * PART : (p + 1) * PART]
+        return blocks.at[index[0], index[1], index[2], core, pl.ds(*PARTS[p])]
 
     def stage(p, k):
         ref = region(p, k, False)
@@ -441,31 +482,41 @@
             lanes = slice((2 * a + b) * 256, (2 * a + b + 1) * 256)
             for t in range(4):
                 big_x[t * BIG_W : (t + 1) * BIG_W, lanes] = blocks[a, b, t // 2, t % 2, :BIG_W, :256]
-                small_x[t * SMALL_W : (t + 1) * SMALL_W, lanes] = blocks[a, b, t // 2, t % 2, BIG_W:, :256]
+                small_x[t * SMALL_W : (t + 1) * SMALL_W, lanes] = blocks[a, b, t // 2, t % 2, BIG_W:BLOCK, :256]
         lanes = slice(1024 + a * 128, 1024 + (a + 1) * 128)
         for t in range(4):
-            both = blocks[a, 0, t // 2, t % 2, :, 256:] + blocks[a, 1, t // 2, t % 2, :, 256:]
-            big_x[t * BIG_W : (t + 1) * BIG_W, lanes] = both[:BIG_W]
-            small_x[t * SMALL_W : (t + 1) * SMALL_W, lanes] = both[BIG_W:]
-
-    first_step(small_x, small_gram_f32, small_gram, small_poly, small_next)
-    first_step(big_x, big_gram_f32, big_gram, big_poly, big_next)
+            left = blocks[a, 0, t // 2, t % 2, BLOCK:, :].astype(jnp.float32)
+            right = blocks[a, 1, t // 2, t % 2, BLOCK:, :].astype(jnp.float32)
+            for k in range(4):
+                both = jnp.concatenate(
+                    [left[:, k * 64 : (k + 1) * 64], right[:, k * 64 : (k + 1) * 64]], axis=1
+                ).astype(jnp.bfloat16)
+                if k < 3:
+                    big_x[t * BIG_W + k * REST : t * BIG_W + (k + 1) * REST, lanes] = both
+                else:
+                    small_x[t * SMALL_W : (t + 1) * SMALL_W, lanes] = both[:SMALL_W]
+
     main_lanes = pl.ds(pl.multiple_of(place * 256, 256), 256)
     rest_lanes = pl.ds(pl.multiple_of(1024 + z * 128, 128), 128)
-    small_main, small_rest = last_step(
-        small_next, small_gram, slice(None), 4 * SMALL_W, main_lanes, rest_lanes
-    )
+
+    def give_back(results, rows_ref, in_ref, sems):
+        main, rest = results
+        rest = jnp.where(y == 0, rest, pltpu.roll(rest, 64, 1))
+        rows_ref[0:256, :] = main.T.astype(jnp.bfloat16)
+        rows_ref[256:LANES, :] = rest.T.astype(jnp.bfloat16)
+        copy = pltpu.make_async_remote_copy(
+            rows_ref.at[other_rows], in_ref, sems.at[0], sems.at[1], device_id=partner, device_id_type=MESH
+        )
+        copy.start()
+        return copy
+
+    first_step(small_x, small_gram_f32, small_gram, small_poly, small_next)
+    small_results = last_step(small_next, small_gram, slice(None), 4 * SMALL_W, main_lanes, rest_lanes)
+    small_back = give_back(small_results, small_rows, small_in, back_sem.at[1])
+    first_step(big_x, big_gram_f32, big_gram, big_poly, big_next)
     own_columns = pl.ds(pl.multiple_of(tensor * BIG_W, BIG_W), BIG_W)
-    big_main, big_rest = last_step(big_next, big_gram, own_columns, BIG_W, main_lanes, rest_lanes)
-    main = jnp.concatenate([big_main, small_main], axis=0)
-    rest = jnp.concatenate([big_rest, small_rest], axis=0)
-    rest = jnp.where(y == 0, rest, pltpu.roll(rest, 64, 1))
-    result_rows[0:256, :] = main.T.astype(jnp.bfloat16)
-    result_rows[256:LANES, :] = rest.T.astype(jnp.bfloat16)
-    back = pltpu.make_async_remote_copy(
-        result_rows.at[other_rows], result_in, back_sem.at[0], back_sem.at[1], device_id=partner, device_id_type=MESH
-    )
-    back.start()
+    big_results = last_step(big_next, big_gram, own_columns, BIG_W, main_lanes, rest_lanes)
+    back = give_back(big_results, result_rows, result_in, back_sem.at[0])
 
     share = parts[shard]
     for k in range(1, 8):
@@ -482,45 +533,50 @@
     from_blended = 1.0 / (1.0 + momentum_rate)
     from_moment = momentum_rate - momentum_rate * momentum_rate / (1.0 + momentum_rate)
 
-    def row_order(load):
+    def row_order(values):
         low, high = [], []
         for j in range(4):
-            main = load(j // 2, j % 2, slice(0, 256)).astype(jnp.float32)
-            rest = load(j // 2, j % 2, slice(256, LANES)).astype(jnp.float32)
-            if j % 2 == 1:
-                rest = pltpu.roll(rest, 64, 1)
-            low.append(main[:, :ROWS])
-            high.append(jnp.concatenate([main[:, ROWS:], rest[:, :64]], axis=1))
+            low.append(values[:, 256 * j : 256 * j + ROWS])
+            high += [values[:, 256 * j + ROWS : 256 * (j + 1)], values[:, 1024 + 64 * j : 1024 + 64 * (j + 1)]]
         return jnp.concatenate(low + high, axis=1)
 
-    def small_block(a, b, lanes):
-        return jnp.concatenate([blocks[a, b, t // 2, t % 2, BIG_W:, lanes] for t in range(4)], axis=0)
-
-    big_blended = row_order(lambda a, b, lanes: blocks[a, b, x, core, :BIG_W, lanes])
     big_moment_new[0] = jnp.where(
-        big_owner == place, from_blended * big_blended + from_moment * big_moment[0], big_moment[0]
-    )
-    small_blended = row_order(small_block)
+        big_owner == place,
+        from_blended * row_order(big_x[own_columns, :].astype(jnp.float32)) + from_moment * big_moment[0],
+        big_moment[0],
+    )
     small_moment_new[0] = jnp.where(
-        small_owner == place, from_blended * small_blended + from_moment * small_moment[0], small_moment[0]
-    )
-
+        small_owner == place,
+        from_blended * row_order(small_x[...].astype(jnp.float32)) + from_moment * small_moment[0],
+        small_moment[0],
+    )
+
+    small_back.wait_recv()
     back.wait_recv()
-    mine = result_rows[own_rows, :]
-    others = result_in[...]
+    loads[5].wait()
+    loads[6].wait()
     scale = 0.2 * math.sqrt(D)
     for index in range(2):
-        for weight, out, lanes, is_mine in (
-            (big_weight, big_weight_new, slice(0, BIG_W), first_is_mine),
-            (small_weight, small_weight_new, slice(BIG_W, 2 * BIG_W), small_is_mine),
+        for weight, out, rows_ref, in_ref, is_mine in (
+            (small_weight, small_weight_new, small_rows, small_in, small_is_mine),
+            (big_weight, big_weight_new, result_rows, result_in, first_is_mine),
         ):
             update = jnp.where(
-                is_mine == (index == 0), mine[:, lanes].astype(jnp.float32), others[:, lanes].astype(jnp.float32)
+                is_mine == (index == 0), rows_ref[own_rows, :].astype(jnp.float32), in_ref[...].astype(jnp.float32)
             )
             values = weight[index].astype(jnp.float32)
             out[index] = (values - muon_rate * (scale * update + weight_decay * values)).astype(jnp.bfloat16)
-    for copy in [swap, own_copy, back] + moves + vec_moves + sent + forwarded:
+    for copy in [swap, own_copy, small_back, back] + moves + vec_moves + sent + forwarded:
         copy.wait_send()
+
+
+def store_kernel(*refs):
+    sems = refs[8]
+    copies = [pltpu.make_async_copy(refs[k], refs[4 + k], sems.at[k]) for k in range(4)]
+    for copy in copies:
+        copy.start()
+    for copy in copies:
+        copy.wait()
 
 
 def per_device(
@@ -539,6 +595,7 @@
     entries = vec_param.shape[0]
     shards = lax.axis_size("shard")
     vmem = pl.BlockSpec(memory_space=pltpu.VMEM)
+    hbm = pl.BlockSpec(memory_space=pl.ANY)
     rows = jax.ShapeDtypeStruct((1, entries), jnp.float32)
     out_shape = (
         jax.ShapeDtypeStruct(big_weight.shape, jnp.bfloat16),
@@ -555,14 +612,22 @@
     outs = pl.pallas_call(
         muon_kernel,
         out_shape=out_shape,
-        in_specs=[pl.BlockSpec(memory_space=pltpu.SMEM)] + [vmem] * 10,
+        in_specs=[pl.BlockSpec(memory_space=pltpu.SMEM)] + [hbm] * 7 + [vmem] * 3,
         out_specs=(vmem,) * 7,
         scratch_shapes=[
+            pltpu.VMEM(big_grad.shape, bf16),
+            pltpu.VMEM(big_weight.shape, bf16),
+            pltpu.VMEM(big_moment.shape, f32),
+            pltpu.VMEM(small_grad.shape, bf16),
+            pltpu.VMEM(small_weight.shape, bf16),
+            pltpu.VMEM(small_moment.shape, f32),
+            pltpu.VMEM((shards, 1, entries), f32),
+            dma((7,)),
             pltpu.VMEM((LANES, 256), bf16),
             pltpu.VMEM((ROWS, 256), bf16),
-            pltpu.VMEM((4, BLOCK, LANES), bf16),
-            pltpu.VMEM((4, BLOCK, LANES), bf16),
-            pltpu.VMEM((2, 2, 2, 2, BLOCK, LANES), bf16),
+            pltpu.VMEM((4, PACKED, 256), bf16),
+            pltpu.VMEM((4, PACKED, 256), bf16),
+            pltpu.VMEM((2, 2, 2, 2, PACKED, 256), bf16),
             pltpu.VMEM((big, D), bf16),
             pltpu.VMEM((big, D), bf16),
             pltpu.VMEM((small, D), bf16),
@@ -573,8 +638,10 @@
             pltpu.VMEM((small, small), f32),
             pltpu.VMEM((small, small), bf16),
             pltpu.VMEM((small, small), bf16),
-            pltpu.VMEM((LANES, LANES), bf16),
-            pltpu.VMEM((ROWS, LANES), bf16),
+            pltpu.VMEM((LANES, BIG_W), bf16),
+            pltpu.VMEM((ROWS, BIG_W), bf16),
+            pltpu.VMEM((LANES, 4 * SMALL_W), bf16),
+            pltpu.VMEM((ROWS, 4 * SMALL_W), bf16),
             pltpu.VMEM((shards, 1, entries), f32),
             dma((2,)),
             dma((2, 4)),
@@ -583,12 +650,12 @@
             dma((3, 3)),
             dma((3, 3)),
             dma((2,)),
-            dma((2,)),
+            dma((2, 2)),
             dma((8,)),
             dma((8,)),
         ],
         compiler_params=pltpu.CompilerParams(
-            collective_id=0, has_side_effects=True, vmem_limit_bytes=48 * 1024 * 1024
+            collective_id=0, has_side_effects=True, vmem_limit_bytes=60 * 1024 * 1024
         ),
     )(
         owners,
@@ -603,6 +670,14 @@
         vec_first.reshape(1, entries),
         vec_second.reshape(1, entries),
     )
+    outs = list(outs)
+    outs[:4] = pl.pallas_call(
+        store_kernel,
+        out_shape=out_shape[:4],
+        in_specs=[pl.BlockSpec(memory_space=pl.ANY)] * 4,
+        out_specs=(hbm,) * 4,
+        scratch_shapes=[dma((4,))],
+    )(*outs[:4])
     return tuple(outs[:4]) + tuple(value.reshape(entries) for value in outs[4:])
 
 

time: 65.2 us -> 127 us (1.95)
  Pallas kernels: 49.4 us -> 118 us
  local copies, waits for them, and re-layouts: 12 us -> 5.26 us
    pallas_call x0 -> x1, Pallas kernels: none -> 70.6 us  [per_device(): pl.pallas_call(store_kernel, out_shape=out_shape[:4], in_specs=[pl.BlockS...]
    unnamed x24 -> x8, local copies, waits for them, and re-layouts: 11.9 us -> 0.83 us
    pallas_call x1, Pallas kernels: 49.4 us -> 47.8 us  [per_device(): pl.pallas_call(muon_kernel, out_shape=out_shape, in_specs=[pl.BlockSpec(m...]
where the time goes in v2:
time: 127 us; the launch traced here: 126 us
  Pallas kernels  118 us (93%)
  local copies, waits for them, and re-layouts  5.26 us (4%)
  other arithmetic  1.82 us (1%)
    pallas_call x1, Pallas kernels, per_device(): pl.pallas_call(store_kernel, out_shape=out_shape[:4], in_specs=[pl.BlockS...  70.6 us
    pallas_call x1, Pallas kernels, per_device(): pl.pallas_call(muon_kernel, out_shape=out_shape, in_specs=[pl.BlockSpec(m...  47.8 us

profile of v2, /device:TPU:0, one launch (start us, length us, event | category | flops | bytes accessed | tf_op | source)
XLA Modules:
  0.0 126.2 jit_solution(7848198520287224300)
XLA Ops:
  0.6 0.0 copy-start
  0.6 1.3 reshape.36.param
  1.9 1.2 reshape.37.first
  3.1 1.2 reshape.38.second
  4.4 0.0 copy-done
  4.4 0.7 reshape.35.parts_hbm
  5.1 47.8 %shard_map.162 = (bf16[2,160,192]{2,1,0:T(8,128)(2,1)}, f32[1,192,1280]{2,1,0:T(8,128)}, bf16[2,160,192]{2,1,0:T(8,128)(2,1)}, f32[1,192,1280]{2,1,0:T(8,128)}, ...) custom-call(s32[2,2]{1,0:T(2,128)} %owners.1, bf16[2,160,192]{2,1,0:T(8,128)(2,1)} %big_grad_hbm.1, ...), custom_call_target="tpu_custom_call" | custom-call | tf_op jit(solution)/shard_map/pallas_call | solution.py:612
  52.9 70.6 %shard_map.163 = (bf16[2,160,192]{2,1,0:T(8,128)(2,1)}, f32[1,192,1280]{2,1,0:T(8,128)}, bf16[2,160,192]{2,1,0:T(8,128)(2,1)}, f32[1,192,1280]{2,1,0:T(8,128)}) custom-call(bf16[2,160,192]{2,1,0:T(8,128)(2,1)} %get-tuple-element.18.refs_0_, f32[1,192,1280]{2,1,0:T(8,128)} %get-tuple-element.19.refs_1_, bf16[2,160,192]{2,1,0:T(8,128)(2,1)} %get-tuple-element.20.refs_2_, ...), custom_call_target="tpu_custom_call" | custom-call | tf_op jit(solution)/shard_map/pallas_call | solution.py:674
  123.5 0.0 copy-start.3
  123.6 0.7 copy-done.3
  124.2 0.0 copy-start.2
  124.2 0.6 reduce.1
  124.8 0.1 copy-done.2
  124.9 0.0 copy-start.1
  124.9 0.6 reduce.2
  125.5 0.1 copy-done.1
  125.6 0.6 reduce.3
  (1 shorter events, 0.0 us)
Async XLA Ops:
  0.6 3.8 %copy-start = (f32[1,2688]{1,0:T(1,128)S(1)}, f32[1,2688]{1,0:T(1,128)}, u32[]{:S(2)}) copy-start(f32[1,2688]{1,0:T(1,128)} %param.18) | copy-start | bytes 32260
  123.5 0.7 copy-start.3
  124.2 0.7 copy-start.2
  124.9 0.7 copy-start.1

commit v3 on v2

--- a/solution.py
+++ b/solution.py
@@ -570,15 +570,6 @@
         copy.wait_send()
 
 
-def store_kernel(*refs):
-    sems = refs[8]
-    copies = [pltpu.make_async_copy(refs[k], refs[4 + k], sems.at[k]) for k in range(4)]
-    for copy in copies:
-        copy.start()
-    for copy in copies:
-        copy.wait()
-
-
 def per_device(
     big_grad,
     big_weight,
@@ -670,14 +661,6 @@
         vec_first.reshape(1, entries),
         vec_second.reshape(1, entries),
     )
-    outs = list(outs)
-    outs[:4] = pl.pallas_call(
-        store_kernel,
-        out_shape=out_shape[:4],
-        in_specs=[pl.BlockSpec(memory_space=pl.ANY)] * 4,
-        out_specs=(hbm,) * 4,
-        scratch_shapes=[dma((4,))],
-    )(*outs[:4])
     return tuple(outs[:4]) + tuple(value.reshape(entries) for value in outs[4:])
 
 

time: 127 us -> 61.6 us (0.49)
  Pallas kernels: 118 us -> 47.8 us
  local copies, waits for them, and re-layouts: 5.26 us -> 10.2 us
    pallas_call x1 -> x0, Pallas kernels: 70.6 us -> none  [per_device(): pl.pallas_call(store_kernel, out_shape=out_shape[:4], in_specs=[pl.BlockS...]
    unnamed x8 -> x20, local copies, waits for them, and re-layouts: 0.83 us -> 7.77 us
where the time goes in v3:
time: 61.6 us; the launch traced here: 61.2 us
  Pallas kernels  47.8 us (78%)
  local copies, waits for them, and re-layouts  10.2 us (17%)
  other arithmetic  2.52 us (4%)
  between operations  0.67 us (1%)
    pallas_call x1, Pallas kernels, per_device(): pl.pallas_call(muon_kernel, out_shape=out_shape, in_specs=[pl.BlockSpec(m...  47.8 us
    unnamed x20, local copies, waits for them, and re-layouts  7.77 us
    pallas_call x3, other arithmetic, per_device(): pl.pallas_call(muon_kernel, out_shape=out_shape, in_specs=[pl.BlockSpec(m...  1.79 us

profile of v3, /device:TPU:0, one launch (start us, length us, event | category | flops | bytes accessed | tf_op | source)
XLA Modules:
  0.0 61.2 jit_solution(15027921664575035901)
XLA Ops:
  0.6 0.7 %reduce = f32[2688]{0:T(1024)S(1)} reduce(f32[1,2688]{1,0:T(1,128)} %param.18, f32[]{:T(128)} %constant.3), dimensions={0}, to_apply=%param.18.reduce_sub_computation | reduce | bytes 21508 | tf_op args[7]
  1.4 0.0 copy-start.2
  1.4 0.7 %reshape.35.parts_hbm = f32[8,1,336]{2,1,0:T(1,128)} reshape(f32[2688]{0:T(1024)S(1)} %reduce) | data formatting | bytes 21504 | tf_op jit(solution)/shard_map/reshape | solution.py:659
  2.1 0.0 copy-done.2
  2.1 0.0 copy-start.3
  2.1 0.6 reshape.36.param
  2.6 0.1 copy-done.3
  2.8 0.0 copy-start.4
  2.8 0.6 reshape.37.first
  3.3 0.1 copy-done.4
  3.4 0.6 reshape.38.second
  4.0 47.8 %shard_map.162 = (bf16[2,160,192]{2,1,0:T(8,128)(2,1)}, f32[1,192,1280]{2,1,0:T(8,128)}, bf16[2,160,192]{2,1,0:T(8,128)(2,1)}, f32[1,192,1280]{2,1,0:T(8,128)}, ...) custom-call(s32[2,2]{1,0:T(2,128)} %owners.1, bf16[2,160,192]{2,1,0:T(8,128)(2,1)} %big_grad_hbm.1, ...), custom_call_target="tpu_custom_call" | custom-call | tf_op jit(solution)/shard_map/pallas_call | solution.py:603
  51.8 0.0 copy-start.7
  51.8 0.7 %copy-done.7 = f32[1,336]{1,0:T(1,128)S(1)} copy-done((f32[1,336]{1,0:T(1,128)S(1)}, f32[1,336]{1,0:T(1,128)}, u32[]{:S(2)}) %copy-start.7) | copy-done | bytes 1368
  52.5 0.6 reduce.1
  53.1 0.0 copy-start.6
  53.1 0.7 %copy-done.6 = f32[1,336]{1,0:T(1,128)S(1)} copy-done((f32[1,336]{1,0:T(1,128)S(1)}, f32[1,336]{1,0:T(1,128)}, u32[]{:S(2)}) %copy-start.6) | copy-done | bytes 1368
  53.8 0.6 reduce.2
  54.4 0.0 copy-start.5
  54.4 0.7 %copy-done.5 = f32[1,336]{1,0:T(1,128)S(1)} copy-done((f32[1,336]{1,0:T(1,128)S(1)}, f32[1,336]{1,0:T(1,128)}, u32[]{:S(2)}) %copy-start.5) | copy-done | bytes 1368
  55.0 0.6 reduce.3
  55.6 1.6 %copy.22 = bf16[2,160,192]{2,1,0:T(8,128)(2,1)} copy(bf16[2,160,192]{2,1,0:T(8,128)(2,1)} %get-tuple-element.28) | data formatting | bytes 245760
  57.2 0.0 copy-start.1
  57.2 0.0 copy-start
  57.2 2.3 %copy.23 = f32[1,192,1280]{2,1,0:T(8,128)} copy(f32[1,192,1280]{2,1,0:T(8,128)} %get-tuple-element.29) | data formatting | bytes 1966080
  59.5 0.0 copy-done.1
  59.5 0.7 %copy.24 = bf16[2,160,192]{2,1,0:T(8,128)(2,1)} copy(bf16[2,160,192]{2,1,0:T(8,128)(2,1)S(1)} %copy-done.1) | data formatting | bytes 245760
  60.2 0.0 copy-done
  60.2 0.9 %copy.25 = f32[1,192,1280]{2,1,0:T(8,128)} copy(f32[1,192,1280]{2,1,0:T(8,128)S(1)} %copy-done) | data formatting | bytes 1966080
Async XLA Ops:
  1.4 0.7 %copy-start.2 = (f32[336]{0:T(512)S(1)}, f32[336]{0:T(512)}, u32[]{:S(2)}) copy-start(f32[336]{0:T(512)} %param.19) | copy-start | bytes 4036
  2.1 0.7 %copy-start.3 = (f32[336]{0:T(512)S(1)}, f32[336]{0:T(512)}, u32[]{:S(2)}) copy-start(f32[336]{0:T(512)} %param.20) | copy-start | bytes 4036
  2.8 0.7 %copy-start.4 = (f32[336]{0:T(512)S(1)}, f32[336]{0:T(512)}, u32[]{:S(2)}) copy-start(f32[336]{0:T(512)} %param.21) | copy-start | bytes 4036
  51.8 0.7 %copy-start.7 = (f32[1,336]{1,0:T(1,128)S(1)}, f32[1,336]{1,0:T(1,128)}, u32[]{:S(2)}) copy-start(f32[1,336]{1,0:T(1,128)} %get-tuple-element.18) | copy-start | bytes 4036
  53.1 0.7 %copy-start.6 = (f32[1,336]{1,0:T(1,128)S(1)}, f32[1,336]{1,0:T(1,128)}, u32[]{:S(2)}) copy-start(f32[1,336]{1,0:T(1,128)} %get-tuple-element.19) | copy-start | bytes 4036
  54.4 0.7 %copy-start.5 = (f32[1,336]{1,0:T(1,128)S(1)}, f32[1,336]{1,0:T(1,128)}, u32[]{:S(2)}) copy-start(f32[1,336]{1,0:T(1,128)} %get-tuple-element.20) | copy-start | bytes 4036
  57.2 2.3 %copy-start.1 = (bf16[2,160,192]{2,1,0:T(8,128)(2,1)S(1)}, bf16[2,160,192]{2,1,0:T(8,128)(2,1)}, u32[]{:S(2)}) copy-start(bf16[2,160,192]{2,1,0:T(8,128)(2,1)} %get-tuple-element.30) | copy-start | bytes 368644
  57.2 3.0 %copy-start = (f32[1,192,1280]{2,1,0:T(8,128)S(1)}, f32[1,192,1280]{2,1,0:T(8,128)}, u32[]{:S(2)}) copy-start(f32[1,192,1280]{2,1,0:T(8,128)} %get-tuple-element.31) | copy-start | bytes 2949124
